TPU v7x, 32 devices: a whole 2x2x4 slice. The times are simulated.
32 devices in a mesh: rows: 8 (over z, y), cols: 4 (over x, core).
Axes of the slice: x: 2, y: 2, z: 4, core: 2. Of those that a mesh axis runs over, the one named last changes fastest.
Arguments:
- tile_values: float32 [120, 256, 256], P('rows'), may hold values from -0.09375 to 0.09375, as said below
- tile_rows: int32 [120], P('rows'), may hold values from 0 to 1
- tile_cols: int32 [120], P('rows'), may hold values from -1 to 15, as said below
- start_vectors: float32 [128, 4096], P('cols', 'rows'), may hold values from -6 to 6
Outputs:
- vectors: float32 [128, 4096], P('cols', 'rows')
- images: float32 [128, 4096], P('cols', 'rows')
Inputs may be any that keep to these rules, and one draw needn't show every extreme that they name: tile_values lie within the stated bounds. `tile_cols`: if slot s of index p of rows is not empty, its column block lies on index p + s // 3 - 2 of rows, that is in 2 * (p + s // 3 - 2) up to 2 * (p + s // 3 - 1) - 1; slots whose index would fall off the mesh are empty.
All inputs are finite; a program needn't handle non-finite values.
Results may differ from a plain program's by a relative error of at most 0.0001.
Values sent between devices are 32-bit elements; how exact they have to be, the bound alone decides.
A program may use at most 64 MiB of HBM per device.

v0:
```python
import functools

import jax
import jax.numpy as jnp
from jax import lax
from jax.experimental import pallas as pl
from jax.experimental.pallas import tpu as pltpu
from jax.sharding import PartitionSpec as P

REACH = 2
ITERS = 3
PARTS = 3
SUB = 8
GROUPS = 2 * REACH + 1
MESH = pl.DeviceIdType.MESH
F32 = jnp.float32
BF16 = jnp.bfloat16


def split(x, parts):
    out = []
    for part in range(parts):
        piece = x.astype(BF16)
        out.append(piece)
        if part < parts - 1:
            x = x - piece.astype(F32)
    return out


def dot(a, b, dims):
    return lax.dot_general(a, b, (dims, ((), ())), preferred_element_type=F32)


def dot32(a, b, dims):
    return lax.dot_general(
        a, b, (dims, ((), ())), precision=lax.Precision.HIGHEST, preferred_element_type=F32
    )


def wait_bytes(ref, sem):
    pltpu.make_async_copy(ref, ref, sem).wait()


def factor_step(m_ref, step):
    size = m_ref.shape[0]
    base = pl.multiple_of(step * SUB, SUB)
    lane = lax.broadcasted_iota(jnp.int32, (SUB, size), 1) - base
    row = lax.broadcasted_iota(jnp.int32, (SUB, size), 0)
    band = m_ref[pl.ds(base, SUB), :]
    turned = pltpu.roll(band, lax.rem(size - base, size), 1)
    cols = [jnp.broadcast_to(turned[:, k : k + 1], (SUB, size)) for k in range(SUB)]
    inverse_rows = jnp.zeros((SUB, size), F32)
    for k in range(SUB):
        inverse = 1.0 / jnp.broadcast_to(cols[k][k : k + 1, :], (SUB, size))
        inverse_rows = jnp.where(row == k, inverse, inverse_rows)
        if k < SUB - 1:
            scale = jnp.where(row > k, cols[k] * inverse, 0.0)
            for other in range(k + 1, SUB):
                cols[other] = cols[other] - scale * cols[other][k : k + 1, :]
            pivot = jnp.where(lane[:1] == k, 1.0, band[k : k + 1, :])
            band = jnp.where((lane == k) & (row > k), 0.0, band) - scale * pivot
    right = jnp.where(lane == row, 1.0, jnp.where((lane > row) & (lane < SUB), 0.0, band))
    left = jnp.where(lane >= SUB, band * inverse_rows, 0.0)
    left_parts = [part.astype(F32) for part in split(left, 3)]
    right_parts = [part.astype(F32) for part in split(right, 3)]
    pairs = [(0, 0), (0, 1), (1, 0), (1, 1), (0, 2), (2, 0)]
    left_all = jnp.concatenate([left_parts[a] for a, b in pairs], axis=0).astype(BF16)
    right_all = jnp.concatenate([right_parts[b] for a, b in pairs], axis=0).astype(BF16)
    change = dot(left_all, right_all, ((0,), (0,)))
    whole_lane = lax.broadcasted_iota(jnp.int32, (size, size), 1) - base
    whole_row = lax.broadcasted_iota(jnp.int32, (size, size), 0) - base
    cleared = (whole_row >= SUB) & (whole_lane >= 0) & (whole_lane < SUB)
    m_ref[...] = jnp.where(cleared, 0.0, m_ref[...]) - change
    m_ref[pl.ds(base, SUB), :] = band


def inverse_factor(m_ref, scale):
    size = m_ref.shape[0]

    def step(index, carry):
        factor_step(m_ref, index)
        return carry

    lax.fori_loop(0, size // SUB, step, 0)
    lane = lax.broadcasted_iota(jnp.int32, (size, size), 1)
    row = lax.broadcasted_iota(jnp.int32, (size, size), 0)
    whole = m_ref[...]
    pivots = jnp.sum(jnp.where(lane == row, whole, 0.0), axis=1, keepdims=True)
    unit = jnp.where(lane == row, 1.0, jnp.where(lane < row, whole, 0.0))
    m_ref[...] = unit * (scale / jnp.sqrt(pivots))


def kernel(
    n_rows, n_cols, scale,
    tiles_hbm, tile_rows, tile_cols, start,
    vectors_out, images_out,
    tiles, dense, source, window, terms, landed, gram, collected, whole_gram, all_images, all_pulled,
    tile_sem, window_send, window_recv, terms_send, terms_recv,
    reduce_send, reduce_recv, spread_send, spread_recv, last_send, last_recv,
):
    p, c = lax.axis_index("rows"), lax.axis_index("cols")
    n_devices = n_rows * n_cols
    me = p * n_cols + c
    local, width = start.shape
    piece = width // n_cols
    size = local * n_cols
    blocks = 2
    tile = tiles.shape[1]
    in_group = tiles.shape[0] // GROUPS
    reducers = size // SUB
    stride = n_devices // reducers
    is_reducer = lax.rem(me, stride) == 0

    def at(row, col):
        return {"rows": row, "cols": col}

    def flat(index):
        return at(index // n_cols, lax.rem(index, n_cols))

    def valid(group):
        there = p + group - REACH
        return (there >= 0) & (there < n_rows)

    def copy_of_tiles(group):
        part = pl.ds(group * in_group, in_group)
        return pltpu.make_async_copy(tiles_hbm.at[part], tiles.at[part], tile_sem.at[group])

    for group in range(GROUPS):
        copy_of_tiles(group).start()

    barrier = pltpu.get_barrier_semaphore()

    def greet(index, carry):
        @pl.when(index != me)
        def _():
            pl.semaphore_signal(barrier, inc=1, device_id=flat(index), device_id_type=MESH)

        return carry

    lax.fori_loop(0, n_devices, greet, 0)

    for part in range(n_cols):
        source[0, part] = start[:, part * piece : (part + 1) * piece]
    for group in range(GROUPS):

        @pl.when(jnp.logical_not(valid(group)))
        def _():
            for iteration in range(ITERS):
                part = pl.ds(group * n_cols, n_cols)
                window[iteration, part] = jnp.zeros((n_cols, local, piece), F32)
                terms[iteration, part] = jnp.zeros((n_cols, local, piece), F32)

    pl.semaphore_wait(barrier, n_devices - 1)

    for group in range(GROUPS):
        mirror = GROUPS - 1 - group
        there = window.at[0, pl.ds(mirror * n_cols, n_cols)]
        if group == REACH:
            pltpu.make_async_copy(source.at[0], there, window_recv.at[0, mirror]).start()
        else:

            @pl.when(valid(group))
            def _():
                pltpu.make_async_remote_copy(
                    src_ref=source.at[0],
                    dst_ref=there,
                    send_sem=window_send.at[0, group],
                    recv_sem=window_recv.at[0, mirror],
                    device_id=at(p + group - REACH, c),
                    device_id_type=MESH,
                ).start()

    chunk = 32
    chunks = tile // chunk
    for group in range(GROUPS):
        copy_of_tiles(group).wait()
        weights = []
        for r in range(blocks):
            for b in range(blocks):
                for s in range(in_group):
                    slot = group * in_group + s
                    hit = (tile_rows[slot] == r) & (lax.rem(tile_cols[slot], blocks) == b)
                    weights.append(jnp.where(hit, 1.0, 0.0).astype(F32))

        def build(index, carry):
            start_row = pl.multiple_of(index * chunk, chunk)
            values = [tiles[group * in_group + s, pl.ds(start_row, chunk), :] for s in range(in_group)]
            for r in range(blocks):
                for b in range(blocks):
                    first = (r * blocks + b) * in_group
                    total = values[0] * weights[first]
                    for s in range(1, in_group):
                        total = total + values[s] * weights[first + s]
                    for number, part in enumerate(split(total, PARTS)):
                        dense[number, group, pl.ds(r * tile + start_row, chunk), b * tile : (b + 1) * tile] = part
            return carry

        lax.fori_loop(0, chunks, build, 0)

    def product(x, group, dims):
        parts = split(x, PARTS)
        total = None
        for number in range(PARTS):
            count = PARTS - number
            stacked = jnp.concatenate(parts[:count], axis=0)
            result = dot(stacked, dense[number, group], dims)
            for k in range(count):
                term = result[k * local : (k + 1) * local]
                total = term if total is None else total + term
        return total

    def send_pieces(iteration, group, buffer, sources, first, send, recv):
        mirror = GROUPS - 1 - group
        slot = mirror * n_cols + c
        for col in range(n_cols):

            def remote():
                pltpu.make_async_remote_copy(
                    src_ref=sources.at[first + col],
                    dst_ref=buffer.at[iteration, slot],
                    send_sem=send.at[iteration, group],
                    recv_sem=recv.at[iteration, mirror],
                    device_id=at(p + group - REACH, col),
                    device_id_type=MESH,
                ).start()

            if group == REACH:
                pl.when(col != c)(remote)

                @pl.when(col == c)
                def _():
                    pltpu.make_async_copy(
                        sources.at[first + col], buffer.at[iteration, slot], recv.at[iteration, mirror]
                    ).start()
            else:
                pl.when(valid(group))(remote)

    def spread_over_cols(src, buffer, number):
        for col in range(n_cols):

            @pl.when(col != c)
            def _():
                pltpu.make_async_remote_copy(
                    src_ref=src,
                    dst_ref=buffer.at[c],
                    send_sem=last_send.at[number],
                    recv_sem=last_recv.at[number],
                    device_id=at(p, col),
                    device_id_type=MESH,
                ).start()

            @pl.when(col == c)
            def _():
                pltpu.make_async_copy(src, buffer.at[c], last_recv.at[number]).start()

    order = [group for group in range(GROUPS) if group != REACH]
    order = sorted(order, key=lambda group: -abs(group - REACH)) + [REACH]

    def wait_group(buffer, recv, iteration, group):
        part = buffer.at[iteration, pl.ds(group * n_cols, n_cols)]
        pl.when(valid(group))(lambda: wait_bytes(part, recv.at[iteration, group]))

    def images_and_terms(iteration):
        images = jnp.zeros((local, width), F32)
        for group in reversed(order):
            wait_group(window, window_recv, iteration, group)
            near = jnp.concatenate([window[iteration, group * n_cols + k] for k in range(n_cols)], axis=1)
            images = images + product(near, group, ((1,), (1,)))
        if iteration == ITERS - 1:
            images_out[...] = images
            spread_over_cols(images_out, all_images, 0)
        for group in order:
            pulled = product(images, group, ((1,), (0,)))
            for col in range(n_cols):
                landed[iteration, group * n_cols + col] = pulled[:, col * piece : (col + 1) * piece]
            send_pieces(
                iteration, group, terms, landed.at[iteration], group * n_cols, terms_send, terms_recv
            )

    def pull(iteration):
        total = None
        for group in order:
            wait_group(terms, terms_recv, iteration, group)
            part = terms[iteration, group * n_cols : (group + 1) * n_cols].reshape(size, piece)
            total = part if total is None else total + part
        return total

    def start_gram(iteration, pulled):
        gram[iteration] = dot32(pulled, pulled, ((1,), (1,)))

        def send(index, carry):
            part = gram.at[iteration, pl.ds(pl.multiple_of(index * SUB, SUB), SUB)]

            @pl.when(index * stride != me)
            def _():
                pltpu.make_async_remote_copy(
                    src_ref=part,
                    dst_ref=collected.at[iteration, me],
                    send_sem=reduce_send.at[iteration],
                    recv_sem=reduce_recv.at[iteration],
                    device_id=flat(index * stride),
                    device_id_type=MESH,
                ).start()

            @pl.when(index * stride == me)
            def _():
                pltpu.make_async_copy(part, collected.at[iteration, me], reduce_recv.at[iteration]).start()

            return carry

        lax.fori_loop(0, reducers, send, 0)

    def spread_gram(iteration):
        @pl.when(is_reducer)
        def _():
            wait_bytes(collected.at[iteration], reduce_recv.at[iteration])
            mine = pl.ds(pl.multiple_of(me // stride * SUB, SUB), SUB)
            whole_gram[ITERS + iteration, mine] = jnp.sum(collected[iteration], axis=0)
            part = whole_gram.at[ITERS + iteration, mine]
            target = whole_gram.at[iteration, mine]

            def send(index, carry):
                @pl.when(index != me)
                def _():
                    pltpu.make_async_remote_copy(
                        src_ref=part,
                        dst_ref=target,
                        send_sem=spread_send.at[iteration],
                        recv_sem=spread_recv.at[iteration],
                        device_id=flat(index),
                        device_id_type=MESH,
                    ).start()

                return carry

            pltpu.make_async_copy(part, target, spread_recv.at[iteration]).start()
            lax.fori_loop(0, n_devices, send, 0)

    def factor(iteration):
        wait_bytes(whole_gram.at[iteration], spread_recv.at[iteration])
        inverse_factor(whole_gram.at[iteration], scale)

    for iteration in range(ITERS):
        if iteration > 0:
            spread_gram(iteration - 1)
        images_and_terms(iteration)
        if iteration > 0:
            factor(iteration - 1)
        pulled = pull(iteration)
        if iteration > 0:
            pulled = dot32(whole_gram[iteration - 1], pulled, ((1,), (0,)))
        source[iteration + 1] = pulled.reshape(n_cols, local, piece)
        if iteration < ITERS - 1:
            for group in order:
                send_pieces(
                    iteration + 1, group, window, source.at[iteration + 1], 0, window_send, window_recv
                )
        start_gram(iteration, pulled)
        if iteration == ITERS - 1:
            spread_over_cols(source.at[ITERS], all_pulled, 1)

    spread_gram(ITERS - 1)
    own = pl.ds(pl.multiple_of(c * local, local), local)
    wait_bytes(all_images, last_recv.at[0])
    wait_bytes(all_images.at[pl.ds(0, n_cols - 1)], last_send.at[0])
    images_out[...] = dot32(
        whole_gram[ITERS - 2, own], all_images[...].reshape(size, width), ((1,), (0,))
    )
    factor(ITERS - 1)
    wait_bytes(all_pulled, last_recv.at[1])
    mix = whole_gram[ITERS - 1, own]
    for part in range(n_cols):
        vectors_out[:, part * piece : (part + 1) * piece] = dot32(
            mix, all_pulled[part].reshape(size, piece), ((1,), (0,))
        )

    wait_bytes(all_pulled.at[pl.ds(0, n_cols - 1)], last_send.at[1])
    for iteration in range(ITERS):
        for group in range(GROUPS):
            for buffer, send in ((window, window_send), (terms, terms_send)):
                if group == REACH:
                    if buffer is window and iteration == 0:
                        continue
                    part = buffer.at[iteration, pl.ds(0, n_cols - 1)]
                    wait_bytes(part, send.at[iteration, group])
                else:
                    part = buffer.at[iteration, pl.ds(0, n_cols)]
                    pl.when(valid(group))(functools.partial(wait_bytes, part, send.at[iteration, group]))

        @pl.when(is_reducer)
        def _():
            wait_bytes(gram.at[iteration, pl.ds(0, size - SUB)], reduce_send.at[iteration])
            wait_bytes(collected.at[iteration, pl.ds(0, n_devices - 1)], spread_send.at[iteration])

        @pl.when(jnp.logical_not(is_reducer))
        def _():
            wait_bytes(gram.at[iteration], reduce_send.at[iteration])


def solution(mesh):
    n_rows, n_cols = mesh.shape["rows"], mesh.shape["cols"]

    def body(tile_values, tile_rows, tile_cols, start_vectors):
        slots, tile = tile_values.shape[:2]
        local, width = start_vectors.shape
        size, piece = local * n_cols, width // n_cols
        scale = float((width * n_rows) ** 0.5)
        pieces = (ITERS, GROUPS * n_cols, local, piece)
        dma = pltpu.SemaphoreType.DMA
        vmem = pl.BlockSpec(memory_space=pltpu.VMEM)
        smem = pl.BlockSpec(memory_space=pltpu.SMEM)
        out = jax.ShapeDtypeStruct((local, width), F32)
        return pl.pallas_call(
            functools.partial(kernel, n_rows, n_cols, scale),
            out_shape=(out, out),
            in_specs=[pl.BlockSpec(memory_space=pl.ANY), smem, smem, vmem],
            out_specs=(vmem, vmem),
            scratch_shapes=[
                pltpu.VMEM((slots, tile, tile), F32),
                pltpu.VMEM((PARTS, GROUPS, width, width), BF16),
                pltpu.VMEM((ITERS + 1, n_cols, local, piece), F32),
                pltpu.VMEM(pieces, F32),
                pltpu.VMEM(pieces, F32),
                pltpu.VMEM(pieces, F32),
                pltpu.VMEM((ITERS, size, size), F32),
                pltpu.VMEM((ITERS, n_rows * n_cols, SUB, size), F32),
                pltpu.VMEM((2 * ITERS, size, size), F32),
                pltpu.VMEM((n_cols, local, width), F32),
                pltpu.VMEM((n_cols, n_cols, local, piece), F32),
                dma((GROUPS,)),
                dma((ITERS, GROUPS)),
                dma((ITERS, GROUPS)),
                dma((ITERS, GROUPS)),
                dma((ITERS, GROUPS)),
                dma((ITERS,)),
                dma((ITERS,)),
                dma((ITERS,)),
                dma((ITERS,)),
                dma((2,)),
                dma((2,)),
            ],
            compiler_params=pltpu.CompilerParams(
                collective_id=0, has_side_effects=True, vmem_limit_bytes=48 * 1024 * 1024
            ),
        )(tile_values, tile_rows, tile_cols, start_vectors)

    return jax.shard_map(
        body,
        mesh=mesh,
        in_specs=(P("rows", None, None), P("rows"), P("rows"), P("cols", "rows")),
        out_specs=(P("cols", "rows"), P("cols", "rows")),
        check_vma=False,
    )
```

profile of v0, /device:TPU:0, one launch (start us, length us, event | category | flops | bytes accessed | tf_op | source)
XLA Modules:
  0.0 85.3 jit_solution(5145828450214474581)
XLA Ops:
  0.6 0.0 copy-start
  0.6 2.1 %copy-done = f32[15,256,256]{2,1,0:T(8,128)S(1)} copy-done((f32[15,256,256]{2,1,0:T(8,128)S(1)}, f32[15,256,256]{2,1,0:T(8,128)}, u32[]{:S(2)}) %copy-start) | copy-done | bytes 3932184
  2.7 0.0 copy-start.1
  2.7 0.8 copy-done.1
  3.6 0.0 copy-start.2
  3.6 0.7 copy-done.2
  4.2 0.0 copy-start.3
  4.2 0.7 copy-done.3
  4.9 79.1 %shard_map.59 = (f32[32,512]{1,0:T(8,128)S(1)}, f32[32,512]{1,0:T(8,128)S(1)}) custom-call(f32[15,256,256]{2,1,0:T(8,128)S(1)} %copy-done, s32[15]{0:T(128)S(1)} %copy-done.2, s32[15]{0:T(128)S(1)} %copy-done.3, f32[32,512]{1,0:T(8,128)S(1)} %copy-done.1), custom_call_target="tpu_custom_call" | custom-call | tf_op jit(solution)/shard_map/pallas_call | solution.py:413
  84.0 0.6 copy.8
  84.7 0.6 copy.9
Async XLA Ops:
  0.6 2.1 %copy-start = (f32[15,256,256]{2,1,0:T(8,128)S(1)}, f32[15,256,256]{2,1,0:T(8,128)}, u32[]{:S(2)}) copy-start(f32[15,256,256]{2,1,0:T(8,128)} %tiles_hbm.1) | copy-start | bytes 11796484
  2.7 0.8 copy-start.1
  3.6 0.7 copy-start.2
  4.2 0.7 copy-start.3
where the time goes:
time: 85.5 us; the launch traced here: 85.3 us
  Pallas kernels  79.1 us (93%)
  local copies, waits for them, and re-layouts  5.52 us (6%)
    pallas_call x1, Pallas kernels, body(): pl.pallas_call(functools.partial(kernel, n_rows, n_cols, scale), out_shap...  79.1 us
    unnamed x10, local copies, waits for them, and re-layouts  5.52 us

commit v1 on v0

--- a/solution.py
+++ b/solution.py
@@ -9,7 +9,7 @@
 
 REACH = 2
 ITERS = 3
-PARTS = 3
+PARTS = 2
 SUB = 8
 GROUPS = 2 * REACH + 1
 MESH = pl.DeviceIdType.MESH
@@ -41,61 +41,72 @@
     pltpu.make_async_copy(ref, ref, sem).wait()
 
 
-def factor_step(m_ref, step):
-    size = m_ref.shape[0]
-    base = pl.multiple_of(step * SUB, SUB)
-    lane = lax.broadcasted_iota(jnp.int32, (SUB, size), 1) - base
+def inverse_factor(whole, scale):
+    size = whole.shape[0]
+    count = size // SUB
+    bands = [whole[s * SUB : (s + 1) * SUB] for s in range(count)]
+    lane = lax.broadcasted_iota(jnp.int32, (SUB, size), 1)
     row = lax.broadcasted_iota(jnp.int32, (SUB, size), 0)
-    band = m_ref[pl.ds(base, SUB), :]
-    turned = pltpu.roll(band, lax.rem(size - base, size), 1)
-    cols = [jnp.broadcast_to(turned[:, k : k + 1], (SUB, size)) for k in range(SUB)]
-    inverse_rows = jnp.zeros((SUB, size), F32)
-    for k in range(SUB):
-        inverse = 1.0 / jnp.broadcast_to(cols[k][k : k + 1, :], (SUB, size))
-        inverse_rows = jnp.where(row == k, inverse, inverse_rows)
-        if k < SUB - 1:
-            scale = jnp.where(row > k, cols[k] * inverse, 0.0)
-            for other in range(k + 1, SUB):
-                cols[other] = cols[other] - scale * cols[other][k : k + 1, :]
-            pivot = jnp.where(lane[:1] == k, 1.0, band[k : k + 1, :])
-            band = jnp.where((lane == k) & (row > k), 0.0, band) - scale * pivot
-    right = jnp.where(lane == row, 1.0, jnp.where((lane > row) & (lane < SUB), 0.0, band))
-    left = jnp.where(lane >= SUB, band * inverse_rows, 0.0)
-    left_parts = [part.astype(F32) for part in split(left, 3)]
-    right_parts = [part.astype(F32) for part in split(right, 3)]
-    pairs = [(0, 0), (0, 1), (1, 0), (1, 1), (0, 2), (2, 0)]
-    left_all = jnp.concatenate([left_parts[a] for a, b in pairs], axis=0).astype(BF16)
-    right_all = jnp.concatenate([right_parts[b] for a, b in pairs], axis=0).astype(BF16)
-    change = dot(left_all, right_all, ((0,), (0,)))
-    whole_lane = lax.broadcasted_iota(jnp.int32, (size, size), 1) - base
-    whole_row = lax.broadcasted_iota(jnp.int32, (size, size), 0) - base
-    cleared = (whole_row >= SUB) & (whole_lane >= 0) & (whole_lane < SUB)
-    m_ref[...] = jnp.where(cleared, 0.0, m_ref[...]) - change
-    m_ref[pl.ds(base, SUB), :] = band
-
-
-def inverse_factor(m_ref, scale):
-    size = m_ref.shape[0]
-
-    def step(index, carry):
-        factor_step(m_ref, index)
-        return carry
-
-    lax.fori_loop(0, size // SUB, step, 0)
-    lane = lax.broadcasted_iota(jnp.int32, (size, size), 1)
-    row = lax.broadcasted_iota(jnp.int32, (size, size), 0)
-    whole = m_ref[...]
-    pivots = jnp.sum(jnp.where(lane == row, whole, 0.0), axis=1, keepdims=True)
-    unit = jnp.where(lane == row, 1.0, jnp.where(lane < row, whole, 0.0))
-    m_ref[...] = unit * (scale / jnp.sqrt(pivots))
+    full = (SUB, size)
+    result = []
+    for s in range(count):
+        base = s * SUB
+        band = bands[s]
+        cols = [jnp.broadcast_to(band[:, base + k : base + k + 1], full) for k in range(SUB)]
+        entry = {
+            (k, l): jnp.broadcast_to(cols[l][k : k + 1], full) for k in range(SUB) for l in range(k, SUB)
+        }
+        follows = s + 1 < count
+        if follows:
+            below = bands[s + 1]
+            below_cols = [jnp.broadcast_to(below[:, base + k : base + k + 1], full) for k in range(SUB)]
+        inverse_rows = jnp.zeros(full, F32)
+        pivots = jnp.zeros(full, F32)
+        for k in range(SUB):
+            inverse = pl.reciprocal(entry[k, k])
+            pivots = jnp.where(row == k, entry[k, k], pivots)
+            inverse_rows = jnp.where(row == k, inverse, inverse_rows)
+            factors = {l: entry[k, l] * inverse for l in range(k + 1, SUB)}
+            for l in range(k + 1, SUB):
+                for j in range(l, SUB):
+                    entry[l, j] = entry[l, j] - factors[l] * entry[k, j]
+            here = lane == base + k
+            pivot_row = jnp.where(here, 1.0, jnp.broadcast_to(band[k : k + 1], full))
+            if k < SUB - 1:
+                step = jnp.where(row > k, cols[k] * inverse, 0.0)
+                for l in range(k + 1, SUB):
+                    cols[l] = cols[l] - step * entry[k, l]
+                band = jnp.where(here & (row > k), 0.0, band) - step * pivot_row
+            if follows:
+                step = below_cols[k] * inverse
+                for l in range(k + 1, SUB):
+                    below_cols[l] = below_cols[l] - step * entry[k, l]
+                below = jnp.where(here, 0.0, below) - step * pivot_row
+        if follows:
+            bands[s + 1] = below
+        offset = lane - base
+        if s + 2 < count:
+            right = jnp.where(offset == row, 1.0, jnp.where((offset > row) & (offset < SUB), 0.0, band))
+            left_parts = [part.astype(F32) for part in split(band * inverse_rows, 3)]
+            right_parts = [part.astype(F32) for part in split(right, 3)]
+            pairs = [(0, 0), (0, 1), (1, 0), (1, 1), (0, 2), (2, 0)]
+            left_all = jnp.concatenate([left_parts[a] for a, b in pairs], axis=0).astype(BF16)
+            right_all = jnp.concatenate([right_parts[b] for a, b in pairs], axis=0).astype(BF16)
+            change = dot(left_all, right_all, ((0,), (0,)))
+            inside = (offset >= 0) & (offset < SUB)
+            for i in range(s + 2, count):
+                bands[i] = jnp.where(inside, 0.0, bands[i]) - change[i * SUB : (i + 1) * SUB]
+        unit = jnp.where(offset == row, 1.0, jnp.where(offset < row, band, 0.0))
+        result.append(unit * (scale / jnp.sqrt(pivots)))
+    return jnp.concatenate(result, axis=0)
 
 
 def kernel(
     n_rows, n_cols, scale,
-    tiles_hbm, tile_rows, tile_cols, start,
+    tiles_hbm, rows_hbm, cols_hbm, start,
     vectors_out, images_out,
     tiles, dense, source, window, terms, landed, gram, collected, whole_gram, all_images, all_pulled,
-    tile_sem, window_send, window_recv, terms_send, terms_recv,
+    tile_rows, tile_cols, tile_sem, input_sem, window_send, window_recv, terms_send, terms_recv,
     reduce_send, reduce_recv, spread_send, spread_recv, last_send, last_recv,
 ):
     p, c = lax.axis_index("rows"), lax.axis_index("cols")
@@ -128,6 +139,17 @@
     for group in range(GROUPS):
         copy_of_tiles(group).start()
 
+    inputs = [
+        pltpu.make_async_copy(start.at[:, pl.ds(part * piece, piece)], source.at[0, part], input_sem.at[part])
+        for part in range(n_cols)
+    ]
+    tables = [
+        pltpu.make_async_copy(rows_hbm, tile_rows, input_sem.at[n_cols]),
+        pltpu.make_async_copy(cols_hbm, tile_cols, input_sem.at[n_cols + 1]),
+    ]
+    for copy in inputs + tables:
+        copy.start()
+
     barrier = pltpu.get_barrier_semaphore()
 
     def greet(index, carry):
@@ -139,8 +161,6 @@
 
     lax.fori_loop(0, n_devices, greet, 0)
 
-    for part in range(n_cols):
-        source[0, part] = start[:, part * piece : (part + 1) * piece]
     for group in range(GROUPS):
 
         @pl.when(jnp.logical_not(valid(group)))
@@ -150,6 +170,8 @@
                 window[iteration, part] = jnp.zeros((n_cols, local, piece), F32)
                 terms[iteration, part] = jnp.zeros((n_cols, local, piece), F32)
 
+    for copy in inputs:
+        copy.wait()
     pl.semaphore_wait(barrier, n_devices - 1)
 
     for group in range(GROUPS):
@@ -170,6 +192,8 @@
                     device_id_type=MESH,
                 ).start()
 
+    for copy in tables:
+        copy.wait()
     chunk = 32
     chunks = tile // chunk
     for group in range(GROUPS):
@@ -201,7 +225,7 @@
         parts = split(x, PARTS)
         total = None
         for number in range(PARTS):
-            count = PARTS - number
+            count = PARTS
             stacked = jnp.concatenate(parts[:count], axis=0)
             result = dot(stacked, dense[number, group], dims)
             for k in range(count):
@@ -338,7 +362,7 @@
 
     def factor(iteration):
         wait_bytes(whole_gram.at[iteration], spread_recv.at[iteration])
-        inverse_factor(whole_gram.at[iteration], scale)
+        whole_gram[iteration] = inverse_factor(whole_gram[iteration], scale)
 
     for iteration in range(ITERS):
         if iteration > 0:
@@ -408,12 +432,12 @@
         pieces = (ITERS, GROUPS * n_cols, local, piece)
         dma = pltpu.SemaphoreType.DMA
         vmem = pl.BlockSpec(memory_space=pltpu.VMEM)
-        smem = pl.BlockSpec(memory_space=pltpu.SMEM)
+        hbm = pl.BlockSpec(memory_space=pltpu.HBM)
         out = jax.ShapeDtypeStruct((local, width), F32)
         return pl.pallas_call(
             functools.partial(kernel, n_rows, n_cols, scale),
             out_shape=(out, out),
-            in_specs=[pl.BlockSpec(memory_space=pl.ANY), smem, smem, vmem],
+            in_specs=[hbm, hbm, hbm, hbm],
             out_specs=(vmem, vmem),
             scratch_shapes=[
                 pltpu.VMEM((slots, tile, tile), F32),
@@ -427,7 +451,10 @@
                 pltpu.VMEM((2 * ITERS, size, size), F32),
                 pltpu.VMEM((n_cols, local, width), F32),
                 pltpu.VMEM((n_cols, n_cols, local, piece), F32),
+                pltpu.SMEM((slots,), jnp.int32),
+                pltpu.SMEM((slots,), jnp.int32),
                 dma((GROUPS,)),
+                dma((n_cols + 2,)),
                 dma((ITERS, GROUPS)),
                 dma((ITERS, GROUPS)),
                 dma((ITERS, GROUPS)),
@@ -440,7 +467,7 @@
                 dma((2,)),
             ],
             compiler_params=pltpu.CompilerParams(
-                collective_id=0, has_side_effects=True, vmem_limit_bytes=48 * 1024 * 1024
+                collective_id=0, has_side_effects=True, vmem_limit_bytes=62 * 1024 * 1024
             ),
         )(tile_values, tile_rows, tile_cols, start_vectors)
 

time: 85.5 us -> 71.4 us (0.84)
  Pallas kernels: 79.1 us -> 67.6 us
  local copies, waits for them, and re-layouts: 5.52 us -> 2.95 us
    pallas_call x1, Pallas kernels: 79.1 us -> 67.6 us  [body(): pl.pallas_call(functools.partial(kernel, n_rows, n_cols, scale), out_shap...]
    unnamed x10 -> x2, local copies, waits for them, and re-layouts: 5.52 us -> 2.95 us
where the time goes in v1:
time: 71.4 us; the launch traced here: 71.2 us
  Pallas kernels  67.6 us (95%)
  local copies, waits for them, and re-layouts  2.95 us (4%)
    pallas_call x1, Pallas kernels, body(): pl.pallas_call(functools.partial(kernel, n_rows, n_cols, scale), out_shap...  67.6 us
    unnamed x2, local copies, waits for them, and re-layouts  2.95 us

profile of v1, /device:TPU:0, one launch (start us, length us, event | category | flops | bytes accessed | tf_op | source)
XLA Modules:
  0.0 71.2 jit_solution(3832238139650778097)
XLA Ops:
  0.6 67.6 %shard_map.59 = (f32[32,512]{1,0:T(8,128)}, f32[32,512]{1,0:T(8,128)}) custom-call(f32[15,256,256]{2,1,0:T(8,128)} %tiles_hbm.1, s32[15]{0:T(128)} %rows_hbm.1, s32[15]{0:T(128)} %cols_hbm.1, f32[32,512]{1,0:T(8,128)} %start.1), custom_call_target="tpu_custom_call" | custom-call | tf_op jit(solution)/shard_map/pallas_call | solution.py:437
  68.3 1.5 %copy.8 = f32[32,512]{1,0:T(8,128)} copy(f32[32,512]{1,0:T(8,128)} %get-tuple-element.4) | data formatting | bytes 131072
  69.7 1.5 %copy.9 = f32[32,512]{1,0:T(8,128)} copy(f32[32,512]{1,0:T(8,128)} %get-tuple-element.5) | data formatting | bytes 131072

commit v2 on v1

--- a/solution.py
+++ b/solution.py
@@ -11,6 +11,7 @@
 ITERS = 3
 PARTS = 2
 SUB = 8
+VMEM = 62 * 1024 * 1024
 GROUPS = 2 * REACH + 1
 MESH = pl.DeviceIdType.MESH
 F32 = jnp.float32
@@ -41,64 +42,59 @@
     pltpu.make_async_copy(ref, ref, sem).wait()
 
 
-def inverse_factor(whole, scale):
-    size = whole.shape[0]
-    count = size // SUB
-    bands = [whole[s * SUB : (s + 1) * SUB] for s in range(count)]
-    lane = lax.broadcasted_iota(jnp.int32, (SUB, size), 1)
-    row = lax.broadcasted_iota(jnp.int32, (SUB, size), 0)
-    full = (SUB, size)
-    result = []
-    for s in range(count):
-        base = s * SUB
-        band = bands[s]
-        cols = [jnp.broadcast_to(band[:, base + k : base + k + 1], full) for k in range(SUB)]
-        entry = {
-            (k, l): jnp.broadcast_to(cols[l][k : k + 1], full) for k in range(SUB) for l in range(k, SUB)
-        }
-        follows = s + 1 < count
+def factor_step(bands, result, s, scale):
+    count = len(bands)
+    full = bands[0].shape
+    lane = lax.broadcasted_iota(jnp.int32, full, 1)
+    row = lax.broadcasted_iota(jnp.int32, full, 0)
+    base = s * SUB
+    band = bands[s]
+    cols = [jnp.broadcast_to(band[:, base + k : base + k + 1], full) for k in range(SUB)]
+    entry = {
+        (k, l): jnp.broadcast_to(cols[l][k : k + 1], full) for k in range(SUB) for l in range(k, SUB)
+    }
+    follows = s + 1 < count
+    if follows:
+        below = bands[s + 1]
+        below_cols = [jnp.broadcast_to(below[:, base + k : base + k + 1], full) for k in range(SUB)]
+    inverse_rows = jnp.zeros(full, F32)
+    pivots = jnp.zeros(full, F32)
+    for k in range(SUB):
+        inverse = pl.reciprocal(entry[k, k])
+        pivots = jnp.where(row == k, entry[k, k], pivots)
+        inverse_rows = jnp.where(row == k, inverse, inverse_rows)
+        factors = {l: entry[k, l] * inverse for l in range(k + 1, SUB)}
+        for l in range(k + 1, SUB):
+            for j in range(l, SUB):
+                entry[l, j] = entry[l, j] - factors[l] * entry[k, j]
+        here = lane == base + k
+        pivot_row = jnp.where(here, 1.0, jnp.broadcast_to(band[k : k + 1], full))
+        if k < SUB - 1:
+            step = jnp.where(row > k, cols[k] * inverse, 0.0)
+            for l in range(k + 1, SUB):
+                cols[l] = cols[l] - step * entry[k, l]
+            band = jnp.where(here & (row > k), 0.0, band) - step * pivot_row
         if follows:
-            below = bands[s + 1]
-            below_cols = [jnp.broadcast_to(below[:, base + k : base + k + 1], full) for k in range(SUB)]
-        inverse_rows = jnp.zeros(full, F32)
-        pivots = jnp.zeros(full, F32)
-        for k in range(SUB):
-            inverse = pl.reciprocal(entry[k, k])
-            pivots = jnp.where(row == k, entry[k, k], pivots)
-            inverse_rows = jnp.where(row == k, inverse, inverse_rows)
-            factors = {l: entry[k, l] * inverse for l in range(k + 1, SUB)}
+            step = below_cols[k] * inverse
             for l in range(k + 1, SUB):
-                for j in range(l, SUB):
-                    entry[l, j] = entry[l, j] - factors[l] * entry[k, j]
-            here = lane == base + k
-            pivot_row = jnp.where(here, 1.0, jnp.broadcast_to(band[k : k + 1], full))
-            if k < SUB - 1:
-                step = jnp.where(row > k, cols[k] * inverse, 0.0)
-                for l in range(k + 1, SUB):
-                    cols[l] = cols[l] - step * entry[k, l]
-                band = jnp.where(here & (row > k), 0.0, band) - step * pivot_row
-            if follows:
-                step = below_cols[k] * inverse
-                for l in range(k + 1, SUB):
-                    below_cols[l] = below_cols[l] - step * entry[k, l]
-                below = jnp.where(here, 0.0, below) - step * pivot_row
-        if follows:
-            bands[s + 1] = below
-        offset = lane - base
-        if s + 2 < count:
-            right = jnp.where(offset == row, 1.0, jnp.where((offset > row) & (offset < SUB), 0.0, band))
-            left_parts = [part.astype(F32) for part in split(band * inverse_rows, 3)]
-            right_parts = [part.astype(F32) for part in split(right, 3)]
-            pairs = [(0, 0), (0, 1), (1, 0), (1, 1), (0, 2), (2, 0)]
-            left_all = jnp.concatenate([left_parts[a] for a, b in pairs], axis=0).astype(BF16)
-            right_all = jnp.concatenate([right_parts[b] for a, b in pairs], axis=0).astype(BF16)
-            change = dot(left_all, right_all, ((0,), (0,)))
-            inside = (offset >= 0) & (offset < SUB)
-            for i in range(s + 2, count):
-                bands[i] = jnp.where(inside, 0.0, bands[i]) - change[i * SUB : (i + 1) * SUB]
-        unit = jnp.where(offset == row, 1.0, jnp.where(offset < row, band, 0.0))
-        result.append(unit * (scale / jnp.sqrt(pivots)))
-    return jnp.concatenate(result, axis=0)
+                below_cols[l] = below_cols[l] - step * entry[k, l]
+            below = jnp.where(here, 0.0, below) - step * pivot_row
+    if follows:
+        bands[s + 1] = below
+    offset = lane - base
+    if s + 2 < count:
+        right = jnp.where(offset == row, 1.0, jnp.where((offset > row) & (offset < SUB), 0.0, band))
+        left_parts = [part.astype(F32) for part in split(band * inverse_rows, 3)]
+        right_parts = [part.astype(F32) for part in split(right, 3)]
+        pairs = [(0, 0), (0, 1), (1, 0), (1, 1), (0, 2), (2, 0)]
+        left_all = jnp.concatenate([left_parts[a] for a, b in pairs], axis=0).astype(BF16)
+        right_all = jnp.concatenate([right_parts[b] for a, b in pairs], axis=0).astype(BF16)
+        change = dot(left_all, right_all, ((0,), (0,)))
+        inside = (offset >= 0) & (offset < SUB)
+        for i in range(s + 2, count):
+            bands[i] = jnp.where(inside, 0.0, bands[i]) - change[i * SUB : (i + 1) * SUB]
+    unit = jnp.where(offset == row, 1.0, jnp.where(offset < row, band, 0.0))
+    result.append(unit * (scale / jnp.sqrt(pivots)))
 
 
 def kernel(
@@ -152,14 +148,14 @@
 
     barrier = pltpu.get_barrier_semaphore()
 
-    def greet(index, carry):
-        @pl.when(index != me)
-        def _():
-            pl.semaphore_signal(barrier, inc=1, device_id=flat(index), device_id_type=MESH)
-
-        return carry
-
-    lax.fori_loop(0, n_devices, greet, 0)
+    def others(visit):
+        def step(index, carry):
+            visit(flat(lax.rem(me + index, n_devices)))
+            return carry
+
+        lax.fori_loop(1, n_devices, step, 0, unroll=n_devices <= 32)
+
+    others(lambda device: pl.semaphore_signal(barrier, inc=1, device_id=device, device_id_type=MESH))
 
     for group in range(GROUPS):
 
@@ -236,9 +232,10 @@
     def send_pieces(iteration, group, buffer, sources, first, send, recv):
         mirror = GROUPS - 1 - group
         slot = mirror * n_cols + c
-        for col in range(n_cols):
-
-            def remote():
+
+        def remote(steps):
+            for step in steps:
+                col = lax.rem(c + step, n_cols)
                 pltpu.make_async_remote_copy(
                     src_ref=sources.at[first + col],
                     dst_ref=buffer.at[iteration, slot],
@@ -248,34 +245,25 @@
                     device_id_type=MESH,
                 ).start()
 
-            if group == REACH:
-                pl.when(col != c)(remote)
-
-                @pl.when(col == c)
-                def _():
-                    pltpu.make_async_copy(
-                        sources.at[first + col], buffer.at[iteration, slot], recv.at[iteration, mirror]
-                    ).start()
-            else:
-                pl.when(valid(group))(remote)
+        if group == REACH:
+            remote(range(1, n_cols))
+            pltpu.make_async_copy(
+                sources.at[first + c], buffer.at[iteration, slot], recv.at[iteration, mirror]
+            ).start()
+        else:
+            pl.when(valid(group))(functools.partial(remote, range(n_cols)))
 
     def spread_over_cols(src, buffer, number):
-        for col in range(n_cols):
-
-            @pl.when(col != c)
-            def _():
-                pltpu.make_async_remote_copy(
-                    src_ref=src,
-                    dst_ref=buffer.at[c],
-                    send_sem=last_send.at[number],
-                    recv_sem=last_recv.at[number],
-                    device_id=at(p, col),
-                    device_id_type=MESH,
-                ).start()
-
-            @pl.when(col == c)
-            def _():
-                pltpu.make_async_copy(src, buffer.at[c], last_recv.at[number]).start()
+        for step in range(1, n_cols):
+            pltpu.make_async_remote_copy(
+                src_ref=src,
+                dst_ref=buffer.at[c],
+                send_sem=last_send.at[number],
+                recv_sem=last_recv.at[number],
+                device_id=at(p, lax.rem(c + step, n_cols)),
+                device_id_type=MESH,
+            ).start()
+        pltpu.make_async_copy(src, buffer.at[c], last_recv.at[number]).start()
 
     order = [group for group in range(GROUPS) if group != REACH]
     order = sorted(order, key=lambda group: -abs(group - REACH)) + [REACH]
@@ -293,13 +281,24 @@
         if iteration == ITERS - 1:
             images_out[...] = images
             spread_over_cols(images_out, all_images, 0)
-        for group in order:
+        def send(group):
+            send_pieces(
+                iteration, group, terms, landed.at[iteration], group * n_cols, terms_send, terms_recv
+            )
+
+        state = begin_factor(iteration - 1) if iteration > 0 else None
+        for number, group in enumerate(order):
             pulled = product(images, group, ((1,), (0,)))
             for col in range(n_cols):
                 landed[iteration, group * n_cols + col] = pulled[:, col * piece : (col + 1) * piece]
-            send_pieces(
-                iteration, group, terms, landed.at[iteration], group * n_cols, terms_send, terms_recv
-            )
+            if state is None:
+                send(group)
+            else:
+                factor(state, 2 if number == 0 else 1)
+        if state is not None:
+            for group in order:
+                send(group)
+        return state
 
     def pull(iteration):
         total = None
@@ -312,27 +311,27 @@
     def start_gram(iteration, pulled):
         gram[iteration] = dot32(pulled, pulled, ((1,), (1,)))
 
-        def send(index, carry):
-            part = gram.at[iteration, pl.ds(pl.multiple_of(index * SUB, SUB), SUB)]
-
-            @pl.when(index * stride != me)
-            def _():
-                pltpu.make_async_remote_copy(
-                    src_ref=part,
-                    dst_ref=collected.at[iteration, me],
-                    send_sem=reduce_send.at[iteration],
-                    recv_sem=reduce_recv.at[iteration],
-                    device_id=flat(index * stride),
-                    device_id_type=MESH,
-                ).start()
-
-            @pl.when(index * stride == me)
-            def _():
-                pltpu.make_async_copy(part, collected.at[iteration, me], reduce_recv.at[iteration]).start()
-
-            return carry
-
-        lax.fori_loop(0, reducers, send, 0)
+        def part_of(index):
+            return gram.at[iteration, pl.ds(pl.multiple_of(index * SUB, SUB), SUB)]
+
+        def send(index):
+            pltpu.make_async_remote_copy(
+                src_ref=part_of(index),
+                dst_ref=collected.at[iteration, me],
+                send_sem=reduce_send.at[iteration],
+                recv_sem=reduce_recv.at[iteration],
+                device_id=flat(index * stride),
+                device_id_type=MESH,
+            ).start()
+
+        near = me // stride
+        for step in range(1, reducers):
+            send(lax.rem(near + step, reducers))
+        pl.when(jnp.logical_not(is_reducer))(lambda: send(near))
+
+        @pl.when(is_reducer)
+        def _():
+            pltpu.make_async_copy(part_of(near), collected.at[iteration, me], reduce_recv.at[iteration]).start()
 
     def spread_gram(iteration):
         @pl.when(is_reducer)
@@ -343,33 +342,41 @@
             part = whole_gram.at[ITERS + iteration, mine]
             target = whole_gram.at[iteration, mine]
 
-            def send(index, carry):
-                @pl.when(index != me)
-                def _():
-                    pltpu.make_async_remote_copy(
-                        src_ref=part,
-                        dst_ref=target,
-                        send_sem=spread_send.at[iteration],
-                        recv_sem=spread_recv.at[iteration],
-                        device_id=flat(index),
-                        device_id_type=MESH,
-                    ).start()
-
-                return carry
-
             pltpu.make_async_copy(part, target, spread_recv.at[iteration]).start()
-            lax.fori_loop(0, n_devices, send, 0)
-
-    def factor(iteration):
+
+            def send(device):
+                pltpu.make_async_remote_copy(
+                    src_ref=part,
+                    dst_ref=target,
+                    send_sem=spread_send.at[iteration],
+                    recv_sem=spread_recv.at[iteration],
+                    device_id=device,
+                    device_id_type=MESH,
+                ).start()
+
+            others(send)
+
+    steps = size // SUB
+
+    def begin_factor(iteration):
         wait_bytes(whole_gram.at[iteration], spread_recv.at[iteration])
-        whole_gram[iteration] = inverse_factor(whole_gram[iteration], scale)
+        return [whole_gram[iteration, k * SUB : (k + 1) * SUB] for k in range(steps)], []
+
+    def factor(state, count):
+        bands, result = state
+        for _ in range(count):
+            factor_step(bands, result, len(result), scale)
+
+    def end_factor(state, iteration):
+        factor(state, steps - len(state[1]))
+        whole_gram[iteration] = jnp.concatenate(state[1], axis=0)
 
     for iteration in range(ITERS):
         if iteration > 0:
             spread_gram(iteration - 1)
-        images_and_terms(iteration)
+        state = images_and_terms(iteration)
         if iteration > 0:
-            factor(iteration - 1)
+            end_factor(state, iteration - 1)
         pulled = pull(iteration)
         if iteration > 0:
             pulled = dot32(whole_gram[iteration - 1], pulled, ((1,), (0,)))
@@ -390,7 +397,7 @@
     images_out[...] = dot32(
         whole_gram[ITERS - 2, own], all_images[...].reshape(size, width), ((1,), (0,))
     )
-    factor(ITERS - 1)
+    end_factor(begin_factor(ITERS - 1), ITERS - 1)
     wait_bytes(all_pulled, last_recv.at[1])
     mix = whole_gram[ITERS - 1, own]
     for part in range(n_cols):
@@ -421,6 +428,17 @@
             wait_bytes(gram.at[iteration], reduce_send.at[iteration])
 
 
+def hand_over(vectors, images, vectors_out, images_out, sem):
+    copies = [
+        pltpu.make_async_copy(vectors, vectors_out, sem.at[0]),
+        pltpu.make_async_copy(images, images_out, sem.at[1]),
+    ]
+    for copy in copies:
+        copy.start()
+    for copy in copies:
+        copy.wait()
+
+
 def solution(mesh):
     n_rows, n_cols = mesh.shape["rows"], mesh.shape["cols"]
 
@@ -434,7 +452,7 @@
         vmem = pl.BlockSpec(memory_space=pltpu.VMEM)
         hbm = pl.BlockSpec(memory_space=pltpu.HBM)
         out = jax.ShapeDtypeStruct((local, width), F32)
-        return pl.pallas_call(
+        results = pl.pallas_call(
             functools.partial(kernel, n_rows, n_cols, scale),
             out_shape=(out, out),
             in_specs=[hbm, hbm, hbm, hbm],
@@ -467,9 +485,18 @@
                 dma((2,)),
             ],
             compiler_params=pltpu.CompilerParams(
-                collective_id=0, has_side_effects=True, vmem_limit_bytes=62 * 1024 * 1024
+                collective_id=0, has_side_effects=True, vmem_limit_bytes=VMEM
             ),
         )(tile_values, tile_rows, tile_cols, start_vectors)
+        anywhere = pl.BlockSpec(memory_space=pl.ANY)
+        return pl.pallas_call(
+            hand_over,
+            out_shape=(out, out),
+            in_specs=[anywhere, anywhere],
+            out_specs=(anywhere, anywhere),
+            scratch_shapes=[dma((2,))],
+            compiler_params=pltpu.CompilerParams(vmem_limit_bytes=VMEM),
+        )(*results)
 
     return jax.shard_map(
         body,

time: 71.4 us -> 78.4 us (1.098)
  Pallas kernels: 67.6 us -> 77.4 us
  local copies, waits for them, and re-layouts: 2.95 us -> 0 us
    pallas_call x0 -> x1, Pallas kernels: none -> 5.09 us  [body(): pl.pallas_call(hand_over, out_shape=(out, out), in_specs=[anywhere, anywh...]
    pallas_call x1, Pallas kernels: 67.6 us -> 72.3 us  [body(): pl.pallas_call(functools.partial(kernel, n_rows, n_cols, scale), out_shap...]
    unnamed x2 -> x0, local copies, waits for them, and re-layouts: 2.95 us -> none
where the time goes in v2:
time: 78.4 us; the launch traced here: 78.2 us
  Pallas kernels  77.4 us (99%)
  between operations  0.8 us (1%)
    pallas_call x1, Pallas kernels, body(): pl.pallas_call(functools.partial(kernel, n_rows, n_cols, scale), out_shap...  72.3 us
    pallas_call x1, Pallas kernels, body(): pl.pallas_call(hand_over, out_shape=(out, out), in_specs=[anywhere, anywh...  5.09 us

profile of v2, /device:TPU:0, one launch (start us, length us, event | category | flops | bytes accessed | tf_op | source)
XLA Modules:
  0.0 78.2 jit_solution(7296557002137310258)
XLA Ops:
  0.6 72.3 %shard_map.59 = (f32[32,512]{1,0:T(8,128)}, f32[32,512]{1,0:T(8,128)}) custom-call(f32[15,256,256]{2,1,0:T(8,128)} %tiles_hbm.1, s32[15]{0:T(128)} %rows_hbm.1, s32[15]{0:T(128)} %cols_hbm.1, f32[32,512]{1,0:T(8,128)} %start.1), custom_call_target="tpu_custom_call" | custom-call | tf_op jit(solution)/shard_map/pallas_call | solution.py:455
  72.9 5.1 %shard_map.60 = (f32[32,512]{1,0:T(8,128)}, f32[32,512]{1,0:T(8,128)}) custom-call(f32[32,512]{1,0:T(8,128)} %get-tuple-element.4.vectors, f32[32,512]{1,0:T(8,128)} %get-tuple-element.5.images), custom_call_target="tpu_custom_call" | custom-call | tf_op jit(solution)/shard_map/pallas_call | solution.py:492
